TPU v7x, 256 devices: a whole 4x4x8 slice. The times are simulated.
256 devices in a mesh: row: 16 (over x_hi, z), col: 16 (over x_lo, y, core).
Axes of the slice: x: 4 (x_hi: 2, x_lo: 2; x = x_hi * 2 + x_lo), y: 4, z: 8, core: 2. Of those that a mesh axis runs over, the one named last changes fastest.
Arguments:
- pair_state: bfloat16 [512, 512, 128], P('row', 'col'), may hold values from -6 to 6
- valid_tokens: int32 [1], replicated, may hold values from 256 to 512
- proj_weight: bfloat16 [128, 512], replicated, may hold values from -0.5 to 0.5
- gate_weight: bfloat16 [128, 128], replicated, may hold values from -0.5 to 0.5
- out_weight: bfloat16 [128, 128], replicated, may hold values from -0.5 to 0.5
- up_weight: bfloat16 [128, 1024], replicated, may hold values from -0.5 to 0.5
- down_weight: bfloat16 [512, 128], replicated, may hold values from -0.25 to 0.25
- gate_scales: float32 [3, 128], replicated, may hold values from 0.5 to 2
- hidden_scales: float32 [512], replicated, may hold values from 0.5 to 2
- cotangent: bfloat16 [512, 512, 128], P('row', 'col'), may hold values from -8 to 8
Outputs:
- layer_out: bfloat16 [512, 512, 128], P('row', 'col')
- gate_grads: float32 [3, 128], replicated
- hidden_grads: float32 [512], replicated
All inputs are finite; a program needn't handle non-finite values.
Results may differ from a plain program's by a relative error of at most 0.015.
Values may be sent and summed in bfloat16 or wider, within the bound.
A program may use at most 128 MiB of HBM per device.

v0:
```python
import jax
import jax.numpy as jnp
from jax import lax
from jax.sharding import PartitionSpec as P

epsilon = 1e-05


def layer_norm(values):
    average = jnp.mean(values, axis=-1, keepdims=True)
    centred = values - average
    inverse_std = lax.rsqrt(jnp.mean(centred * centred, axis=-1, keepdims=True) + epsilon)
    return (centred * inverse_std, inverse_std)


def norm_backward(gradient, normed, inverse_std):
    grad_mean = jnp.mean(gradient, axis=-1, keepdims=True)
    cross_mean = jnp.mean(gradient * normed, axis=-1, keepdims=True)
    return inverse_std * (gradient - grad_mean - normed * cross_mean)


def linear_map(values, weight):
    flattened = values.reshape(-1, values.shape[-1])
    result = jnp.dot(flattened, weight, preferred_element_type=jnp.float32)
    return result.reshape(values.shape[:-1] + (weight.shape[1],))


def linear_back(values, weight):
    flattened = values.reshape(-1, values.shape[-1])
    result = lax.dot_general(
        flattened, weight, (((1,), (1,)), ((), ())), preferred_element_type=jnp.float32
    )
    return result.reshape(values.shape[:-1] + (weight.shape[0],))


def project_inputs(pair_state, pair_mask, proj_weight, gate_weight, gate_scales):
    channels = pair_state.shape[-1]
    normed = layer_norm(pair_state.astype(jnp.float32))[0].astype(jnp.bfloat16)
    projected = linear_map(normed, proj_weight)
    value_left = projected[..., :channels]
    value_right = projected[..., channels : 2 * channels]
    logit_left = projected[..., 2 * channels : 3 * channels]
    logit_right = projected[..., 3 * channels :]
    sigma_left = jax.nn.sigmoid(gate_scales[0] * logit_left)
    sigma_right = jax.nn.sigmoid(gate_scales[1] * logit_right)
    left_proj = (pair_mask * sigma_left * value_left).astype(jnp.bfloat16)
    right_proj = (pair_mask * sigma_right * value_right).astype(jnp.bfloat16)
    left_slope = (pair_mask * value_left * sigma_left * (1.0 - sigma_left) * logit_left).astype(
        jnp.bfloat16
    )
    right_slope = (
        pair_mask * value_right * sigma_right * (1.0 - sigma_right) * logit_right
    ).astype(jnp.bfloat16)
    gate_logit = linear_map(normed, gate_weight)
    gate_value = jax.nn.sigmoid(gate_scales[2] * gate_logit)
    return (left_proj, right_proj, left_slope, right_slope, gate_logit, gate_value)


def finish(
    pair_state,
    triangle,
    gate_logit,
    gate_value,
    out_weight,
    up_weight,
    down_weight,
    hidden_scales,
    cotangent,
):
    tri_hat, tri_inverse = layer_norm(triangle)
    tri_normed = tri_hat.astype(jnp.bfloat16)
    out_proj = linear_map(tri_normed, out_weight)
    middle = (pair_state.astype(jnp.float32) + gate_value * out_proj).astype(jnp.bfloat16)
    middle = lax.optimization_barrier(middle)
    middle_full = middle.astype(jnp.float32)
    mid_hat, mid_inverse = layer_norm(middle_full)
    mid_normed = mid_hat.astype(jnp.bfloat16)
    upward = linear_map(mid_normed, up_weight)
    hidden_width = hidden_scales.shape[0]
    first_half = upward[..., :hidden_width]
    second_half = upward[..., hidden_width:]
    activated = jax.nn.silu(first_half)
    product = activated * second_half
    hidden = (hidden_scales * product).astype(jnp.bfloat16)
    layer_out = (middle_full + linear_map(hidden, down_weight)).astype(jnp.bfloat16)
    hidden_grad = linear_back(cotangent, down_weight)
    hidden_term = jnp.sum(hidden_grad * product, axis=(0, 1))
    sigma_first = jax.nn.sigmoid(first_half)
    scaled = hidden_grad * hidden_scales
    grad_first = scaled * second_half * sigma_first * (1.0 + first_half * (1.0 - sigma_first))
    grad_second = scaled * activated
    grad_upward = jnp.concatenate([grad_first, grad_second], axis=-1).astype(jnp.bfloat16)
    grad_mid = cotangent.astype(jnp.float32) + norm_backward(
        linear_back(grad_upward, up_weight), mid_hat, mid_inverse
    )
    gate_term = jnp.sum(
        grad_mid * out_proj * gate_value * (1.0 - gate_value) * gate_logit, axis=(0, 1)
    )
    grad_outproj = (grad_mid * gate_value).astype(jnp.bfloat16)
    triangle_grad = norm_backward(
        linear_back(grad_outproj, out_weight), tri_hat, tri_inverse
    ).astype(jnp.bfloat16)
    return (layer_out, triangle_grad, gate_term, hidden_term)


def shards(
    pair_state,
    valid_tokens,
    proj_weight,
    gate_weight,
    out_weight,
    up_weight,
    down_weight,
    gate_scales,
    hidden_scales,
    cotangent,
):
    row_count = pair_state.shape[0]
    col_count = pair_state.shape[1]
    row_anchor = lax.axis_index("row") * row_count
    col_anchor = lax.axis_index("col") * col_count
    token_limit = valid_tokens[0]
    keep_rows = (row_anchor + jnp.arange(row_count, dtype=jnp.int32) < token_limit).astype(
        jnp.float32
    )
    keep_cols = (col_anchor + jnp.arange(col_count, dtype=jnp.int32) < token_limit).astype(
        jnp.float32
    )
    pair_mask = keep_rows[:, None, None] * keep_cols[None, :, None]
    left_proj, right_proj, left_slope, right_slope, gate_logit, gate_value = project_inputs(
        pair_state, pair_mask, proj_weight, gate_weight, gate_scales
    )
    right_panel = lax.all_gather(right_proj, "row", axis=0, tiled=True)
    swapped = lax.psum_scatter(
        jnp.einsum("jkc,ikc->jic", right_panel, left_proj, preferred_element_type=jnp.float32),
        "col",
        scatter_dimension=0,
        tiled=True,
    )
    triangle = jnp.transpose(swapped, (1, 0, 2))
    layer_out, triangle_grad, gate_term, hidden_term = finish(
        pair_state,
        triangle,
        gate_logit,
        gate_value,
        out_weight,
        up_weight,
        down_weight,
        hidden_scales,
        cotangent,
    )
    grad_panel = lax.all_gather(triangle_grad, "col", axis=1, tiled=True)
    grad_left = jnp.einsum(
        "ijc,jkc->ikc", grad_panel, right_panel, preferred_element_type=jnp.float32
    )
    left_term = jnp.sum(grad_left * left_slope, axis=(0, 1))
    grad_right = lax.psum_scatter(
        jnp.einsum(
            "ijc,ikc->jkc", grad_panel, left_proj, preferred_element_type=jnp.float32
        ).astype(jnp.bfloat16),
        "row",
        scatter_dimension=0,
        tiled=True,
    ).astype(jnp.float32)
    right_term = jnp.sum(grad_right * right_slope, axis=(0, 1))
    gate_terms = jnp.stack([left_term, right_term, gate_term])
    gate_grads, hidden_grads = lax.psum((gate_terms, hidden_term), ("row", "col"))
    return (layer_out, gate_grads, hidden_grads)


def solution(mesh):
    return jax.shard_map(
        shards,
        mesh=mesh,
        in_specs=(
            P("row", "col", None),
            P(),
            P(),
            P(),
            P(),
            P(),
            P(),
            P(),
            P(),
            P("row", "col", None),
        ),
        out_specs=(P("row", "col", None), P(), P()),
        check_vma=False,
    )
```

profile of v0, /device:TPU:1, one launch (start us, length us, event | category | flops | bytes accessed | tf_op | source)
XLA Modules:
  0.0 584.4 jit_solution(14163318657208647236)
XLA Ops:
  7.2 0.0 copy-start
  7.2 0.0 all-gather.3.cloned.1.call-start
  7.9 0.8 slice_bitcast_fusion.2
  8.7 1.2 convert_reduce_fusion.1
  9.9 1.3 fusion.19
  11.2 0.1 broadcast_multiply_fusion
  11.3 1.5 fusion.36
  12.8 1.1 multiply_convert_fusion.8
  13.9 0.0 all-gather.3.cloned.1.call-update
  13.9 0.0 reduce-scatter.3.cloned.1.call-start
  14.0 2.7 copy.30
  16.6 98.0 %all-gather.3.cloned.1.call-done = bf16[512,32,128]{2,1,0:T(8,128)(2,1)} async-done(((bf16[32,32,128]{2,1,0:T(8,128)(2,1)}), bf16[512,32,128]{2,1,0:T(8,128)(2,1)}) %all-gather.3.cloned.1.call-update) | async-done | bytes 4194320 | tf_op jit(solution)/shard_map/all_gather | solution.py:133
  114.6 8.6 %copy.27 = bf16[512,32,128]{0,1,2:T(8,128)(2,1)} copy(bf16[512,32,128]{2,1,0:T(8,128)(2,1)} %all-gather.3.cloned.1.call-done) | data formatting | bytes 8388608 | tf_op jit(solution)/shard_map/all_gather | solution.py:133
  123.2 6.7 %convolution_bitcast_fusion = f32[512,32,128]{0,1,2:T(8,128)} fusion(bf16[32,32,128]{0,1,2:T(8,128)(2,1)S(1)} %copy.30, bf16[512,32,128]{0,1,2:T(8,128)(2,1)} %copy.27), kind=kOutput, calls=%fused_computation.1 | convolution fusion | flops 134217728 | bytes 12845056 | tf_op jit(solution)/shard_map/jkc,ikc->jic/dot_general | solution.py:135
  129.9 11.0 %copy.24 = f32[512,32,128]{2,1,0:T(8,128)} copy(f32[512,32,128]{0,1,2:T(8,128)} %convolution_bitcast_fusion) | data formatting | bytes 16777216 | tf_op jit(solution)/shard_map/jkc,ikc->jic/transpose | solution.py:135
  140.9 0.0 reduce-scatter.3.cloned.1.call-update
  140.9 0.0 all-gather.5.cloned.1.call-start
  140.9 0.7 copy-done.12
  141.6 2.2 fusion.38
  143.8 70.3 %reduce-scatter.3.cloned.1.call-done = f32[32,32,128]{2,1,0:T(8,128)} async-done(((f32[512,32,128]{2,1,0:T(8,128)}), f32[32,32,128]{2,1,0:T(8,128)}) %reduce-scatter.3.cloned.1.call-update) | async-done | bytes 524304 | tf_op jit(solution)/shard_map/reduce_scatter | solution.py:134
  214.1 1.4 bitcast_reduce_fusion
  215.5 1.6 multiply_reduce_fusion.4
  217.1 0.0 copy-done.15
  217.1 2.6 fusion.21
  219.8 0.2 convert_reduce_fusion
  220.0 0.4 fusion.18
  220.4 0.0 copy-done
  220.4 0.0 copy-start.10
  220.4 0.0 copy-start.13
  220.4 0.0 copy-start.16
  220.4 0.8 fusion.28
  221.2 0.1 copy-done.10
  221.4 0.0 copy-done.13
  221.4 0.0 copy-done.16
  221.4 1.4 multiply_convert_fusion.1
  222.8 0.5 copy-done.4
  223.3 0.8 fusion.51
  224.1 0.0 copy-start.9
  224.2 0.2 copy-done.3
  224.4 0.2 copy-done.7
  224.5 1.7 fusion.50
  226.2 0.0 copy-done.9
  226.3 0.6 multiply_convert_fusion.6
  226.9 0.8 copy.26
  227.7 0.0 all-gather.5.cloned.1.call-update
  227.7 0.2 reduce-scatter.5.cloned.1.call-start
  227.9 42.6 %all-gather.5.cloned.1.call-done = bf16[32,512,128]{2,0,1:T(8,128)(2,1)} async-done(((bf16[32,32,128]{2,0,1:T(8,128)(2,1)}), bf16[32,512,128]{2,0,1:T(8,128)(2,1)}) %all-gather.5.cloned.1.call-update) | async-done | bytes 4194320 | tf_op jit(solution)/shard_map/all_gather | solution.py:152
  270.6 8.6 %copy.28 = bf16[32,512,128]{1,0,2:T(8,128)(2,1)} copy(bf16[32,512,128]{2,0,1:T(8,128)(2,1)} %all-gather.5.cloned.1.call-done) | data formatting | bytes 8388608 | tf_op jit(solution)/shard_map/all_gather | solution.py:152
  279.2 5.4 fusion.53
  284.5 9.2 %copy.32 = bf16[128,32,512]{0,1,2:T(8,128)(2,1)} copy(bf16[128,32,512]{2,1,0:T(8,128)(2,1)} %fusion.53) | data formatting | bytes 8388608 | tf_op jit(solution)/shard_map/ijc,ikc->jkc/dot_general | solution.py:158
  293.7 0.0 reduce-scatter.5.cloned.1.call-update
  293.8 0.0 copy-start.14
  293.8 0.9 copy-done.6
  294.7 0.2 copy-done.8
  294.9 0.1 copy-done.11
  294.9 1.8 multiply_reduce_fusion.1
  296.7 3.8 fusion.5
  300.6 0.0 copy-done.1
  300.6 1.0 copy-done.2
  301.5 2.6 fusion.52
  304.1 2.8 copy.29
  306.9 190.7 %reduce-scatter.5.cloned.1.call-done = bf16[32,32,128]{2,1,0:T(8,128)(2,1)} async-done(((bf16[512,32,128]{2,1,0:T(8,128)(2,1)}), bf16[32,32,128]{2,1,0:T(8,128)(2,1)}) %reduce-scatter.5.cloned.1.call-update) | async-done | bytes 262160 | tf_op jit(solution)/shard_map/reduce_scatter | solution.py:157
  497.7 1.4 fusion.22
  499.1 78.8 %all-reduce = (f32[3,128]{1,0:T(4,128)}, f32[512]{0:T(512)}) all-reduce(f32[3,128]{1,0:T(4,128)S(1)} %pad_maximum_fusion, f32[512]{0:T(512)S(1)} %get-tuple-element.13), channel_id=1, replica_groups=mesh['row'=16,'col'=16] {'row','col'}, use_global_device_ids=true, to_apply=%region_15.16 | all-reduce | flops 896 | bytes 7168 | tf_op jit(solution)/shard_map/psum | solution.py:167
  (25 shorter events, 0.1 us)
Async XLA Ops:
  7.2 213.2 %copy-start = (bf16[128,1024]{1,0:T(8,128)(2,1)S(1)}, bf16[128,1024]{1,0:T(8,128)(2,1)}, u32[]{:S(2)}) copy-start(bf16[128,1024]{1,0:T(8,128)(2,1)} %param.15) | copy-start | bytes 786436
  7.2 107.4 %all-gather.3.cloned.1.call-start = ((), (), s32[]{:S(2)}) async-start(), calls=%async_computation.2 | async-start | bytes 4456448 | tf_op jit(solution)/shard_map/all_gather | solution.py:133
  13.9 200.2 %reduce-scatter.3.cloned.1.call-start = ((), (), s32[]{:S(2)}) async-start(), calls=%async_computation.3 | async-start | bytes 8912896 | tf_op jit(solution)/shard_map/reduce_scatter | solution.py:134
  140.9 0.8 copy-start.12
  140.9 76.3 %copy-start.15 = (bf16[128,128]{1,0:T(8,128)(2,1)S(1)}, bf16[128,128]{1,0:T(8,128)(2,1)}, u32[]{:S(2)}) copy-start(bf16[128,128]{1,0:T(8,128)(2,1)} %param.14) | copy-start | bytes 98308
  140.9 129.7 %all-gather.5.cloned.1.call-start = ((), (), s32[]{:S(2)}) async-start(), calls=%async_computation.4 | async-start | bytes 4456448 | tf_op jit(solution)/shard_map/all_gather | solution.py:152
  219.8 4.4 copy-start.5
  220.4 1.0 copy-start.10
  220.4 1.0 copy-start.13
  220.4 1.0 copy-start.16
  221.4 1.9 copy-start.4
  223.3 1.0 copy-start.3
  223.3 1.2 copy-start.7
  224.1 2.1 copy-start.9
  227.7 269.9 %reduce-scatter.5.cloned.1.call-start = ((), (), s32[]{:S(2)}) async-start(), calls=%async_computation.5 | async-start | bytes 4456448 | tf_op jit(solution)/shard_map/reduce_scatter | solution.py:157
  293.7 0.9 copy-start.6
  293.7 1.1 copy-start.8
  293.7 1.2 copy-start.11
  293.8 2.9 copy-start.14
  296.7 3.9 copy-start.1
  296.7 4.8 copy-start.2
Sparse Core Ops, SparseCore 0:
  14.0 100.5 all-gather.2
  141.0 73.0 reduce-scatter.2
  227.8 42.6 all-gather.4
  293.9 203.7 reduce-scatter.4
where the time goes:
time: 586 us; the launch traced here: 584 us
  waiting for transfers between devices  402 us (69%)
  blocking collectives  78.8 us (13%)
  local copies, waits for them, and re-layouts  48.3 us (8%)
  matrix products  29.5 us (5%)
  between operations  14.7 us (3%)
  other arithmetic  11.1 us (2%)
    reduce_scatter x1, waiting for transfers between devices, shards(): lax.psum_scatter(jnp.einsum('ijc,ikc->jkc', grad_panel, left_proj, prefer...  191 us
    all_gather x1, waiting for transfers between devices, shards(): right_panel = lax.all_gather(right_proj, 'row', axis=0, tiled=True)  98 us
    psum x1, blocking collectives, shards(): lax.psum((gate_terms, hidden_term), ('row', 'col'))  78.8 us
    reduce_scatter x1, waiting for transfers between devices, shards(): lax.psum_scatter(jnp.einsum('jkc,ikc->jic', right_panel, left_proj, prefe...  70.3 us
    all_gather x1, waiting for transfers between devices, shards(): grad_panel = lax.all_gather(triangle_grad, 'col', axis=1, tiled=True)  42.6 us
  transfers between devices with their start and end apart: 4, of which 4 were waited for; matrix products, arithmetic and copies ran while one was open for 3% of the time, Pallas kernels for 0%

commit v1 on v0

v1 whole, which is shorter than its diff:
```python
import functools

import jax
import jax.numpy as jnp
from jax import lax
from jax.experimental import pallas as pl
from jax.experimental.pallas import tpu as pltpu
from jax.sharding import PartitionSpec as P

F32, BF16 = jnp.float32, jnp.bfloat16
EPS = 1e-5
MESH = pl.DeviceIdType.MESH
C = 128
BLK = 32
SA = 65
ST = 33


def mm(a, b):
    return jnp.dot(a, b, preferred_element_type=F32)


def mm_nt(a, b):
    return lax.dot_general(a, b, (((1,), (1,)), ((), ())), preferred_element_type=F32)


def sigmoid(v):
    return 0.5 * jnp.tanh(0.5 * v) + 0.5


def norm(v):
    centred = v - jnp.mean(v, axis=-1, keepdims=True)
    inverse = lax.rsqrt(jnp.mean(centred * centred, axis=-1, keepdims=True) + EPS)
    return centred * inverse, inverse


def norm_back(g, hat, inverse):
    g_mean = jnp.mean(g, axis=-1, keepdims=True)
    cross = jnp.mean(g * hat, axis=-1, keepdims=True)
    return inverse * (g - g_mean - hat * cross)


class Copies:
    def __init__(self, send, recv):
        self.send, self.recv, self.count, self.table = send, recv, 0, {}

    def start(self, name, src, dst, device, when=None):
        copy = pltpu.make_async_remote_copy(
            src_ref=src,
            dst_ref=dst,
            send_sem=self.send.at[self.count],
            recv_sem=self.recv.at[self.count],
            device_id=device,
            device_id_type=MESH,
        )
        self.count += 1
        self.table[name] = (copy, when)
        if when is None:
            copy.start()
        else:
            pl.when(when)(copy.start)

    def wait_recv(self, name):
        copy, when = self.table[name]
        if when is None:
            copy.wait_recv()
        else:
            pl.when(when)(copy.wait_recv)

    def wait_sends(self):
        for copy, when in self.table.values():
            if when is None:
                copy.wait_send()
            else:
                pl.when(when)(copy.wait_send)


N_COPIES = 47


def project(pan, blocks, quad, w_ref, s_ref, out):
    def step(n, carry):
        i = n * 2
        x = jnp.concatenate([pan[b, i + m] for m in range(2) for b in blocks], axis=0)
        p = mm_nt(w_ref[...], x)
        for m in range(2):
            value, logit = p[:C, m * 128 : (m + 1) * 128], p[C:, m * 128 : (m + 1) * 128]
            sig = 0.5 * jnp.tanh(s_ref[...] * logit) + 0.5
            proj = sig * value
            slope = proj * (logit * (1.0 - sig))
            out[quad, pl.ds(i + m, C, stride=SA), :] = proj
            out[quad, pl.ds(i + m + BLK, C, stride=SA), :] = slope
        return carry

    lax.fori_loop(0, BLK // 2, step, 0)


def products(a_ref, b_ref, t_ref):
    def step(n, carry):
        for m in range(4):
            ch = n * 4 + m
            rows = pl.ds(ch * SA, 2 * BLK)
            a = jnp.concatenate([a_ref[q, rows, :].astype(BF16) for q in range(4)], axis=1)
            b = jnp.concatenate([b_ref[q, rows, :].astype(BF16) for q in range(4)], axis=1)
            t = mm_nt(a, b)
            t_ref[pl.ds(ch * ST, BLK), :] = jnp.concatenate([t[:BLK], t[BLK:]], axis=1)
        return carry

    lax.fori_loop(0, C // 4, step, 0)


def finish(x_ref, cot_ref, gate_w, out_w, up_w, down_w, gs_ref, hs_ref, t_ref, out_ref, vec_ref, tri, tri_l, tri_r, acc):
    def turn(i, carry):
        t = t_ref[pl.ds(i, C, stride=ST), :].T
        rows = pl.ds(pl.multiple_of(i * BLK, BLK), BLK)
        tri[rows, :] = t[:BLK]
        tri_r[rows, :] = t[BLK : 2 * BLK]
        tri_l[rows, :] = t[2 * BLK : 3 * BLK]
        return carry

    lax.fori_loop(0, BLK, turn, 0)
    acc[...] = jnp.zeros_like(acc)
    n_rows = 8
    n_pos = n_rows * BLK
    gs = gs_ref[2:3, :]
    hs = hs_ref[...]

    def chunk(n, carry):
        own = pl.ds(n * n_rows, n_rows)
        rows = pl.ds(pl.multiple_of(n * n_pos, n_pos), n_pos)
        x = x_ref[own].reshape(n_pos, C).astype(F32)
        cot = cot_ref[own].reshape(n_pos, C)
        gate_logit = mm(norm(x)[0].astype(BF16), gate_w[...])
        gate = sigmoid(gs * gate_logit)
        tri_hat, tri_inv = norm(tri[rows, :])
        out_proj = mm(tri_hat.astype(BF16), out_w[...])
        middle = (x + gate * out_proj).astype(BF16).astype(F32)
        mid_hat, mid_inv = norm(middle)
        upward = mm(mid_hat.astype(BF16), up_w[...])
        first, second = upward[:, :512], upward[:, 512:]
        s = sigmoid(first)
        act = first * s
        product = act * second
        layer_out = middle + mm((hs * product).astype(BF16), down_w[...])
        out_ref[own] = layer_out.astype(BF16).reshape(n_rows, BLK, C)
        hidden_grad = mm_nt(cot, down_w[...])
        hidden = jnp.sum(hidden_grad * product, axis=0, keepdims=True)
        scaled = hidden_grad * hs
        g_first = scaled * second * s * (1.0 + first * (1.0 - s))
        g_second = scaled * act
        g_up = jnp.concatenate([g_first.astype(BF16), g_second.astype(BF16)], axis=1)
        g_mid = cot.astype(F32) + norm_back(mm_nt(g_up, up_w[...]), mid_hat, mid_inv)
        gate_term = jnp.sum(g_mid * out_proj * gate * (1.0 - gate) * gate_logit, axis=0, keepdims=True)
        g_out = (g_mid * gate).astype(BF16)
        t_grad = norm_back(mm_nt(g_out, out_w[...]), tri_hat, tri_inv).astype(BF16).astype(F32)
        left = jnp.sum(t_grad * tri_l[rows, :], axis=0, keepdims=True)
        right = jnp.sum(t_grad * tri_r[rows, :], axis=0, keepdims=True)
        parts = [left, right, gate_term] + [hidden[:, m * C : (m + 1) * C] for m in range(4)]
        for m, part in enumerate(parts):
            acc[m : m + 1, :] += part
        return carry

    lax.fori_loop(0, BLK // n_rows, chunk, 0)
    vec_ref[...] = acc[...]


def layer_kernel(
    x_ref, valid_ref, proj_w, gate_w, out_w, up_w, down_w, gs_ref, hs_ref, cot_ref,
    out_ref, vec_ref,
    lpan, rpan, a_ref, b_ref, t_ref, tri, tri_l, tri_r, acc, wa, wb, sa, sb, send, recv,
):
    r, c = lax.axis_index("row"), lax.axis_index("col")
    xh, z = r // 8, r % 8
    xl, y, core = c // 8, (c // 2) % 4, c % 2

    def row_of(h, dz):
        return h * 8 + (z + dz) % 8

    def col_of(h, dy, k):
        return (h * 4 + (y + dy) % 4) * 2 + k

    across = (c, r)
    far = (row_of(1 - xh, 0), c)
    up, down = (row_of(xh, 1), c), (row_of(xh, 7), c)
    sibling = (r, col_of(xl, 0, 1 - core))
    near = (r, col_of(1 - xl, 0, core))
    along = [(r, col_of(xl, d, core)) for d in (1, 2, 3)]
    off = r != c

    barrier = pltpu.get_barrier_semaphore()
    partners = [far, up, down, sibling, near] + along
    for device in partners:
        pl.semaphore_signal(barrier, inc=1, device_id=device, device_id_type=MESH)

    @pl.when(off)
    def _():
        pl.semaphore_signal(barrier, inc=1, device_id=across, device_id_type=MESH)

    limit = valid_ref[0]
    rows_i = lax.broadcasted_iota(jnp.int32, (BLK, BLK, C), 0) + r * BLK
    rows_k = lax.broadcasted_iota(jnp.int32, (BLK, BLK, C), 1) + c * BLK
    keep = jnp.where(jnp.maximum(rows_i, rows_k) < limit, 1.0, 0.0)
    normed = (norm(x_ref[...].astype(F32))[0] * keep).astype(BF16)
    lpan[c] = normed

    @pl.when(jnp.logical_not(off))
    def _():
        rpan[r] = normed

    pl.semaphore_wait(barrier, len(partners) + jnp.where(off, 1, 0))

    cp = Copies(send, recv)
    halves = (pl.ds(0, 16), pl.ds(16, 16))

    def r_copy(name, slot, half, device):
        ref = rpan.at[slot, halves[half]]
        cp.start(name, ref, ref, device)

    def l_copy(name, slot, device):
        ref = lpan.at[slot]
        cp.start(name, ref, ref, device)

    for half in range(2):
        cp.start(("t", half), lpan.at[c, halves[half]], rpan.at[c, halves[half]], across, off)
    l_copy("near", c, near)
    for d in range(3):
        l_copy(("y", d, 0), c, along[d])
    l_copy("sib", c, sibling)

    for w_ref, s_ref, side in ((wa, sa, 0), (wb, sb, 1)):
        w_ref[:C, :] = proj_w[:, side * C : (side + 1) * C].T
        w_ref[C:, :] = proj_w[:, (side + 2) * C : (side + 3) * C].T
        s_ref[...] = jnp.broadcast_to(0.5 * gs_ref[side : side + 1, :], (C, C)).T

    for half in range(2):
        cp.wait_recv(("t", half))
        r_copy(("up", 1, half), r, half, up)
        r_copy(("down", 1, half), r, half, down)
        r_copy(("far", half), r, half, far)
    cp.wait_recv("near")
    for d in range(3):
        l_copy(("y", d, 1), col_of(1 - xl, 0, core), along[d])
    l_copy("sibnear", col_of(1 - xl, 0, core), sibling)
    cp.wait_recv(("far", 0))
    r_copy(("up", 1, 2), row_of(1 - xh, 0), 0, up)
    r_copy(("down", 1, 2), row_of(1 - xh, 0), 0, down)

    items = {"up": {1: (0, 1, 2), 2: (0, 1, 2), 3: (0, 1, 2), 4: (0, 2)}, "down": {1: (0, 1, 2), 2: (0, 1, 2), 3: (0, 1, 2), 4: (1,)}}

    def hop(h):
        for item in range(3):
            for flow, sign, device in (("up", -1, up), ("down", 1, down)):
                if item not in items[flow][h]:
                    continue
                cp.wait_recv((flow, h, item))
                slot = row_of(1 - xh if item == 2 else xh, sign * h + 8)
                if h < 4 and item in items[flow][h + 1]:
                    r_copy((flow, h + 1, item), slot, item % 2, device)
                if item == 1:
                    r_copy(("cross", flow, h), slot, 1, far)

    def l_hop(part):
        for d in range(3):
            cp.wait_recv(("y", d, part))
            slot = col_of(1 - xl if part else xl, 3 - d, core)
            l_copy(("sib", d, part), slot, sibling)

    hop(1)
    l_hop(0)
    hop(2)
    l_hop(1)
    for name in ["sib", "sibnear"] + [("sib", d, part) for part in range(2) for d in range(3)]:
        cp.wait_recv(name)
    hop(3)
    hop(4)
    cp.wait_recv(("far", 1))
    for flow, last in (("up", 3), ("down", 4)):
        for h in range(1, last + 1):
            cp.wait_recv(("cross", flow, h))

    order = [0, 7, 1, 6, 2, 5, 3, 4]
    quads = [[row_of(h, dz) for dz in order[2 * q : 2 * q + 2] for h in range(2)] for q in range(4)]
    for q in range(4):
        project(lpan, quads[q], q, wa, sa, a_ref)
        project(rpan, quads[q], q, wb, sb, b_ref)
    products(a_ref, b_ref, t_ref)
    finish(x_ref, cot_ref, gate_w, out_w, up_w, down_w, gs_ref, hs_ref, t_ref, out_ref, vec_ref, tri, tri_l, tri_r, acc)
    cp.wait_sends()
    assert cp.count == N_COPIES


def sum_kernel(v_ref, o_ref, slots, send, recv):
    r, c = lax.axis_index("row"), lax.axis_index("col")
    xh, z = r // 8, r % 8
    xl, y, core = c // 8, (c // 2) % 4, c % 2
    line = [((xh * 8 + (z + dz) % 8), (c // 2) * 2 + (core + dk) % 2) for dz in range(8) for dk in range(2)]
    plane = [
        (((xh + dh) % 2) * 8 + z, (((xl + dl) % 2) * 4 + (y + dy) % 4) * 2 + core)
        for dh in range(2) for dl in range(2) for dy in range(4)
    ]
    places = (z * 2 + core, (xh * 2 + xl) * 4 + y)
    barrier = pltpu.get_barrier_semaphore()
    for device in line[1:] + plane[1:]:
        pl.semaphore_signal(barrier, inc=1, device_id=device, device_id_type=MESH)
    pl.semaphore_wait(barrier, 30)
    total = v_ref[...]
    for stage, group in enumerate((line, plane)):
        slots[stage, places[stage]] = total
        copies = []
        for n in range(1, 16):
            copy = pltpu.make_async_remote_copy(
                src_ref=slots.at[stage, places[stage]],
                dst_ref=slots.at[stage, places[stage]],
                send_sem=send.at[stage, n],
                recv_sem=recv.at[stage, n],
                device_id=group[n],
                device_id_type=MESH,
            )
            copy.start()
            copies.append(copy)
        for copy in copies:
            copy.wait()
        total = jnp.sum(slots[stage], axis=0)
    o_ref[...] = total


VMEM = pl.BlockSpec(memory_space=pltpu.VMEM)
SMEM = pl.BlockSpec(memory_space=pltpu.SMEM)


def shards(pair_state, valid_tokens, proj_weight, gate_weight, out_weight, up_weight, down_weight, gate_scales, hidden_scales, cotangent):
    panel = pltpu.VMEM((16, BLK, BLK, C), BF16)
    edge = pltpu.VMEM((4, C * SA, 128), F32)
    positions = pltpu.VMEM((BLK * BLK, C), F32)
    layer_out, vector = pl.pallas_call(
        layer_kernel,
        out_shape=(jax.ShapeDtypeStruct((BLK, BLK, C), BF16), jax.ShapeDtypeStruct((8, C), F32)),
        in_specs=[VMEM, SMEM] + [VMEM] * 8,
        out_specs=(VMEM, VMEM),
        scratch_shapes=[
            panel, panel, edge, edge, pltpu.VMEM((C * ST, 128), F32), positions, positions, positions,
            pltpu.VMEM((8, C), F32), pltpu.VMEM((2 * C, C), BF16), pltpu.VMEM((2 * C, C), BF16),
            pltpu.VMEM((C, C), F32), pltpu.VMEM((C, C), F32),
            pltpu.SemaphoreType.DMA((N_COPIES,)), pltpu.SemaphoreType.DMA((N_COPIES,)),
        ],
        compiler_params=pltpu.CompilerParams(collective_id=0, has_side_effects=True, vmem_limit_bytes=60 << 20),
        name="layer",
    )(pair_state, valid_tokens, proj_weight, gate_weight, out_weight, up_weight, down_weight, gate_scales, hidden_scales.reshape(1, 512), cotangent)
    total = pl.pallas_call(
        sum_kernel,
        out_shape=jax.ShapeDtypeStruct((8, C), F32),
        in_specs=[VMEM],
        out_specs=VMEM,
        scratch_shapes=[pltpu.VMEM((2, 16, 8, C), F32), pltpu.SemaphoreType.DMA((2, 16)), pltpu.SemaphoreType.DMA((2, 16))],
        compiler_params=pltpu.CompilerParams(collective_id=1, has_side_effects=True),
        name="sums",
    )(vector)
    return layer_out, total[:3], total[3:7].reshape(512)


def solution(mesh):
    return jax.shard_map(
        shards,
        mesh=mesh,
        in_specs=(P("row", "col", None), P(), P(), P(), P(), P(), P(), P(), P(), P("row", "col", None)),
        out_specs=(P("row", "col", None), P(), P()),
        check_vma=False,
    )
```

time: 586 us -> 140 us (0.24)
  waiting for transfers between devices: 402 us -> 0 us
  Pallas kernels: 0 us -> 135 us
  blocking collectives: 78.8 us -> 0 us
  local copies, waits for them, and re-layouts: 48.3 us -> 3.57 us
  matrix products: 29.5 us -> 0 us
  between operations: 14.7 us -> 1.3 us
  other arithmetic: 11.1 us -> 0 us
    reduce_scatter x2 -> x0, waiting for transfers between devices: 261 us -> none  [the longest x1 191 us: shards(): lax.psum_scatter(jnp.einsum('ijc,ikc->jkc', grad_panel, left_proj, prefer...]
    all_gather x2 -> x0, waiting for transfers between devices: 141 us -> none  [the longest x1 98 us: shards(): right_panel = lax.all_gather(right_proj, 'row', axis=0, tiled=True)]
    pallas_call x0 -> x2, Pallas kernels: none -> 135 us  [the longest x1 120 us: shards(): pl.pallas_call(layer_kernel, out_shape=(jax.ShapeDtypeStruct((BLK, BLK, C...]
    psum x1 -> x0, blocking collectives: 78.8 us -> none  [shards(): lax.psum((gate_terms, hidden_term), ('row', 'col'))]
    dot_general x11 -> x0, matrix products: 29.5 us -> none  [the longest x5 10.9 us: linear_map(): result = jnp.dot(flattened, weight, preferred_element_type=jnp.float32)]
    all_gather x2 -> x0, local copies, waits for them, and re-layouts: 17.2 us -> none  [the longest x1 8.6 us: shards(): grad_panel = lax.all_gather(triangle_grad, 'col', axis=1, tiled=True)]
    dot_general x2 -> x0, local copies, waits for them, and re-layouts: 12 us -> none  [the longest x1 9.2 us: shards(): jnp.einsum('ijc,ikc->jkc', grad_panel, left_proj, preferred_element_type=...]
    transpose x1 -> x0, local copies, waits for them, and re-layouts: 11 us -> none  [shards(): jnp.einsum('jkc,ikc->jic', right_panel, left_proj, preferred_element_type...]
  transfers between devices with their start and end apart: 4 -> 0, of which waited for: 4 -> 0; matrix products, arithmetic and copies ran while one was open for 3% -> 0% of each run, Pallas kernels for 0% -> 0%
where the time goes in v1:
time: 140 us
  Pallas kernels  135 us (96%)
  local copies, waits for them, and re-layouts  3.57 us (3%)
    pallas_call x1, Pallas kernels, shards(): pl.pallas_call(layer_kernel, out_shape=(jax.ShapeDtypeStruct((BLK, BLK, C...  120 us
    pallas_call x1, Pallas kernels, shards(): pl.pallas_call(sum_kernel, out_shape=jax.ShapeDtypeStruct((8, C), F32), i...  15.5 us

profile of v1, /device:TPU:1, one launch (start us, length us, event | category | flops | bytes accessed | tf_op | source)
XLA Modules:
  0.0 140.3 jit_solution(10033948746805460591)
XLA Ops:
  1.3 119.9 %layer.1 = (bf16[32,32,128]{2,1,0:T(8,128)(2,1)}, f32[8,128]{1,0:T(8,128)}) custom-call(bf16[32,32,128]{2,1,0:T(8,128)(2,1)} %x_ref.1, s32[1]{0:T(128)S(6)} %copy.14.valid_ref, bf16[128,512]{1,0:T(8,128)(2,1)} %proj_w.1, bf16[128,128]{1,0:T(8,128)(2,1)} %gate_w.1, bf16[128,128]{1,0:T(8,128)(2,1)} %out_w.1, bf16[128,1024]{1,0:T(8,128)(2,1)} %up_w.1, ...), custom_call_target="tpu_custom_call" | custom-call | tf_op jit(solution)/shard_map/layer/pallas_call | solution.py:335
  121.2 15.5 %sums.1 = f32[8,128]{1,0:T(8,128)} custom-call(f32[8,128]{1,0:T(8,128)} %get-tuple-element.6.v_ref), custom_call_target="tpu_custom_call" | custom-call | tf_op jit(solution)/shard_map/sums/pallas_call | solution.py:349
  136.7 0.0 copy-start
  136.7 1.3 slice_bitcast_fusion
  138.0 0.0 copy-done
  138.0 0.6 slice.6
  138.6 1.7 %copy.15 = bf16[32,32,128]{2,1,0:T(8,128)(2,1)} copy(bf16[32,32,128]{2,1,0:T(8,128)(2,1)} %get-tuple-element.10) | data formatting | bytes 524288
Async XLA Ops:
  136.7 1.3 copy-start

commit v2 on v1

v2 whole, which is shorter than its diff:
```python
import functools

import jax
import jax.numpy as jnp
from jax import lax
from jax.experimental import pallas as pl
from jax.experimental.pallas import tpu as pltpu
from jax.sharding import PartitionSpec as P

F32, BF16 = jnp.float32, jnp.bfloat16
EPS = 1e-5
MESH = pl.DeviceIdType.MESH
C = 128
BLK = 32
SA = 65
GROUP = 16
WIDE = 32
ST = 33


def mm(a, b):
    return jnp.dot(a, b, preferred_element_type=F32)


def mm_nt(a, b):
    return lax.dot_general(a, b, (((1,), (1,)), ((), ())), preferred_element_type=F32)


def sigmoid(v):
    return 0.5 * jnp.tanh(0.5 * v) + 0.5


def norm(v):
    centred = v - jnp.mean(v, axis=-1, keepdims=True)
    inverse = lax.rsqrt(jnp.mean(centred * centred, axis=-1, keepdims=True) + EPS)
    return centred * inverse, inverse


def norm_back(g, hat, inverse):
    g_mean = jnp.mean(g, axis=-1, keepdims=True)
    cross = jnp.mean(g * hat, axis=-1, keepdims=True)
    return inverse * (g - g_mean - hat * cross)


class Copies:
    def __init__(self, send, recv):
        self.send, self.recv, self.count, self.table = send, recv, 0, {}

    def start(self, name, src, dst, device, when=None):
        copy = pltpu.make_async_remote_copy(
            src_ref=src,
            dst_ref=dst,
            send_sem=self.send.at[self.count],
            recv_sem=self.recv.at[self.count],
            device_id=device,
            device_id_type=MESH,
        )
        self.count += 1
        self.table[name] = (copy, when)
        if when is None:
            copy.start()
        else:
            pl.when(when)(copy.start)

    def wait_recv(self, name):
        copy, when = self.table[name]
        if when is None:
            copy.wait_recv()
        else:
            pl.when(when)(copy.wait_recv)

    def wait_sends(self):
        for copy, when in self.table.values():
            if when is None:
                copy.wait_send()
            else:
                pl.when(when)(copy.wait_send)


N_COPIES = 47


def project(pan, blocks, quad, w_ref, s_ref, out):
    def step(n, carry):
        i = n * GROUP
        x = jnp.concatenate([pan[b, i + m] for m in range(GROUP) for b in blocks], axis=0)
        p = mm_nt(w_ref[...], x)
        for m in range(GROUP):
            value, logit = p[:C, m * 128 : (m + 1) * 128], p[C:, m * 128 : (m + 1) * 128]
            sig = 0.5 * jnp.tanh(s_ref[...] * logit) + 0.5
            proj = sig * value
            slope = proj * (logit * (1.0 - sig))
            out[quad, pl.ds(i + m, C, stride=SA), :] = proj
            out[quad, pl.ds(i + m + BLK, C, stride=SA), :] = slope
        return carry

    lax.fori_loop(0, BLK // GROUP, step, 0)


def products(a_ref, b_ref, t_ref):
    def step(n, carry):
        for m in range(WIDE):
            ch = n * WIDE + m
            rows = pl.ds(ch * SA, 2 * BLK)
            a = jnp.concatenate([a_ref[q, rows, :].astype(BF16) for q in range(4)], axis=1)
            b = jnp.concatenate([b_ref[q, rows, :].astype(BF16) for q in range(4)], axis=1)
            t = mm_nt(a, b)
            t_ref[pl.ds(ch * ST, BLK), :] = jnp.concatenate([t[:BLK], t[BLK:]], axis=1)
        return carry

    lax.fori_loop(0, C // WIDE, step, 0)


N_ROWS = 16
N_POS = N_ROWS * BLK


def parts_of(n):
    return pl.ds(n * N_ROWS, N_ROWS), pl.ds(pl.multiple_of(n * N_POS, N_POS), N_POS)


def early(x_ref, cot_ref, gate_w, down_w, gs_ref, logit_ref, gate_ref, hg_ref):
    gs = gs_ref[2:3, :]

    def chunk(n, carry):
        own, rows = parts_of(n)
        x = x_ref[own].reshape(N_POS, C).astype(F32)
        gate_logit = mm(norm(x)[0].astype(BF16), gate_w[...])
        logit_ref[rows, :] = gate_logit
        gate_ref[rows, :] = sigmoid(gs * gate_logit)
        hg_ref[rows, :] = mm_nt(cot_ref[own].reshape(N_POS, C), down_w[...])
        return carry

    lax.fori_loop(0, BLK // N_ROWS, chunk, 0)


def turn(t_ref, tri, tri_l, tri_r):
    def step(n, carry):
        for m in range(4):
            i = n * 4 + m
            t = t_ref[pl.ds(i, C, stride=ST), :].T
            rows = pl.ds(pl.multiple_of(i * BLK, BLK), BLK)
            tri[rows, :] = t[:BLK]
            tri_r[rows, :] = t[BLK : 2 * BLK]
            tri_l[rows, :] = t[2 * BLK : 3 * BLK]
        return carry

    lax.fori_loop(0, BLK // 4, step, 0)


def finish(x_ref, cot_ref, out_w, up_w, down_w, hs_ref, logit_ref, gate_ref, hg_ref, tri, tri_l, tri_r, out_ref, acc):
    acc[...] = jnp.zeros_like(acc)
    hs = hs_ref[...]

    def chunk(n, carry):
        own, rows = parts_of(n)
        x = x_ref[own].reshape(N_POS, C).astype(F32)
        cot = cot_ref[own].reshape(N_POS, C).astype(F32)
        gate_logit, gate, hidden_grad = logit_ref[rows, :], gate_ref[rows, :], hg_ref[rows, :]
        tri_hat, tri_inv = norm(tri[rows, :])
        out_proj = mm(tri_hat.astype(BF16), out_w[...])
        middle = (x + gate * out_proj).astype(BF16).astype(F32)
        mid_hat, mid_inv = norm(middle)
        upward = mm(mid_hat.astype(BF16), up_w[...])
        first, second = upward[:, :512], upward[:, 512:]
        s = sigmoid(first)
        act = first * s
        product = act * second
        layer_out = middle + mm((hs * product).astype(BF16), down_w[...])
        out_ref[own] = layer_out.astype(BF16).reshape(N_ROWS, BLK, C)
        hidden = jnp.sum(hidden_grad * product, axis=0, keepdims=True)
        scaled = hidden_grad * hs
        g_first = scaled * second * s * (1.0 + first * (1.0 - s))
        g_second = scaled * act
        g_up = jnp.concatenate([g_first.astype(BF16), g_second.astype(BF16)], axis=1)
        g_mid = cot + norm_back(mm_nt(g_up, up_w[...]), mid_hat, mid_inv)
        gate_term = jnp.sum(g_mid * out_proj * gate * (1.0 - gate) * gate_logit, axis=0, keepdims=True)
        g_out = (g_mid * gate).astype(BF16)
        t_grad = norm_back(mm_nt(g_out, out_w[...]), tri_hat, tri_inv).astype(BF16).astype(F32)
        left = jnp.sum(t_grad * tri_l[rows, :], axis=0, keepdims=True)
        right = jnp.sum(t_grad * tri_r[rows, :], axis=0, keepdims=True)
        parts = [left, right, gate_term] + [hidden[:, m * C : (m + 1) * C] for m in range(4)]
        for m, part in enumerate(parts):
            acc[m : m + 1, :] += part
        return carry

    lax.fori_loop(0, BLK // N_ROWS, chunk, 0)


def layer_kernel(
    x_ref, valid_ref, proj_w, gate_w, out_w, up_w, down_w, gs_ref, hs_ref, cot_ref,
    out_ref, gate_out, hidden_out,
    lpan, rpan, a_ref, b_ref, t_ref, tri, tri_l, tri_r, logit_ref, gate_ref, hg_ref, acc, wa, wb, sa, sb, slots,
    send, recv, sum_send, sum_recv,
):
    r, c = lax.axis_index("row"), lax.axis_index("col")
    xh, z = r // 8, r % 8
    xl, y, core = c // 8, (c // 2) % 4, c % 2

    def row_of(h, dz):
        return h * 8 + (z + dz) % 8

    def col_of(h, dy, k):
        return (h * 4 + (y + dy) % 4) * 2 + k

    def slot_of(h, dz):
        return h * 8 + (z + dz + 8 - c % 8) % 8

    def col_at(slot):
        return slot // 8 * 8 + slot % 4 * 2 + slot % 8 // 4

    own_slot = slot_of(xh, 0)
    to = (xl * 8 + (z + y + 4 * core) % 8, r)
    sent_slot = xl * 8 + y + 4 * core
    source = (c, col_at(own_slot))
    off = jnp.logical_or(c != r, own_slot % 8 != sent_slot % 8)

    far = (row_of(1 - xh, 0), c)
    up, down = (row_of(xh, 1), c), (row_of(xh, 7), c)
    sibling = (r, col_of(xl, 0, 1 - core))
    near = (r, col_of(1 - xl, 0, core))
    along = [(r, col_of(xl, d, core)) for d in (1, 2, 3)]
    line = [(row_of(xh, dz), col_of(xl, 0, (core + dk) % 2)) for dz in range(8) for dk in range(2)]
    plane = [
        (row_of((xh + dh) % 2, 0), col_of((xl + dl) % 2, dy, core))
        for dh in range(2) for dl in range(2) for dy in range(4)
    ]

    barrier = pltpu.get_barrier_semaphore()
    for device in line[1:] + plane[1:]:
        pl.semaphore_signal(barrier, inc=1, device_id=device, device_id_type=MESH)

    @pl.when(off)
    def _():
        pl.semaphore_signal(barrier, inc=1, device_id=source, device_id_type=MESH)

    limit = valid_ref[0]
    rows_i = lax.broadcasted_iota(jnp.int32, (BLK, BLK, C), 0) + r * BLK
    rows_k = lax.broadcasted_iota(jnp.int32, (BLK, BLK, C), 1) + c * BLK
    keep = jnp.where(jnp.maximum(rows_i, rows_k) < limit, 1.0, 0.0)
    normed = (norm(x_ref[...].astype(F32))[0] * keep).astype(BF16)
    lpan[c] = normed

    @pl.when(jnp.logical_not(off))
    def _():
        rpan[own_slot] = normed

    pl.semaphore_wait(barrier, 30 + jnp.where(off, 1, 0))

    cp = Copies(send, recv)
    halves = (pl.ds(0, 16), pl.ds(16, 16))

    def r_copy(name, slot, half, device):
        ref = rpan.at[slot, halves[half]]
        cp.start(name, ref, ref, device)

    def l_copy(name, slot, device):
        ref = lpan.at[slot]
        cp.start(name, ref, ref, device)

    for half in (1, 0):
        cp.start(("t", half), lpan.at[c, halves[half]], rpan.at[sent_slot, halves[half]], to, off)
    l_copy("near", c, near)
    for d in range(3):
        l_copy(("y", d, 0), c, along[d])
    l_copy("sib", c, sibling)

    for w_ref, s_ref, side in ((wa, sa, 0), (wb, sb, 1)):
        w_ref[:C, :] = proj_w[:, side * C : (side + 1) * C].T
        w_ref[C:, :] = proj_w[:, (side + 2) * C : (side + 3) * C].T
        s_ref[...] = jnp.broadcast_to(0.5 * gs_ref[side : side + 1, :], (C, C)).T
    early(x_ref, cot_ref, gate_w, down_w, gs_ref, logit_ref, gate_ref, hg_ref)

    items = {
        "up": {1: (1, 0, 2), 2: (1, 0, 2), 3: (1, 0, 2), 4: (0, 2)},
        "down": {1: (1, 0, 2), 2: (1, 0, 2), 3: (1, 0, 2), 4: (1,)},
    }
    for half in (1, 0):
        cp.wait_recv(("t", half))
        if half == 0:
            r_copy(("far", 0), own_slot, 0, far)
        r_copy(("up", 1, half), own_slot, half, up)
        r_copy(("down", 1, half), own_slot, half, down)
    r_copy(("far", 1), own_slot, 1, far)
    cp.wait_recv("near")
    for d in range(3):
        l_copy(("y", d, 1), col_of(1 - xl, 0, core), along[d])
    l_copy("sibnear", col_of(1 - xl, 0, core), sibling)
    cp.wait_recv(("far", 0))
    r_copy(("up", 1, 2), slot_of(1 - xh, 0), 0, up)
    r_copy(("down", 1, 2), slot_of(1 - xh, 0), 0, down)

    def hop(h):
        for item in (1, 0, 2):
            for flow, sign, device in (("up", -1, up), ("down", 1, down)):
                if item not in items[flow][h]:
                    continue
                cp.wait_recv((flow, h, item))
                slot = slot_of(1 - xh if item == 2 else xh, sign * h + 8)
                if h < 4 and item in items[flow][h + 1]:
                    r_copy((flow, h + 1, item), slot, item % 2, device)
                if item == 1:
                    r_copy(("cross", flow, h), slot, 1, far)

    def l_hop(part):
        for d in range(3):
            cp.wait_recv(("y", d, part))
            l_copy(("sib", d, part), col_of(1 - xl if part else xl, 3 - d, core), sibling)

    order = [0, 7, 1, 6, 2, 5, 3, 4]
    quads = [[slot_of(h, dz) for dz in order[2 * q : 2 * q + 2] for h in range(2)] for q in range(4)]

    def left(q):
        project(lpan, [col_at(slot) for slot in quads[q]], q, wa, sa, a_ref)

    def right(q):
        project(rpan, quads[q], q, wb, sb, b_ref)

    hop(1)
    l_hop(0)
    hop(2)
    l_hop(1)
    cp.wait_recv(("far", 1))
    cp.wait_recv(("cross", "up", 1))
    right(0)
    for name in ["sib", "sibnear"] + [("sib", d, part) for part in range(2) for d in range(3)]:
        cp.wait_recv(name)
    left(0)
    hop(3)
    cp.wait_recv(("cross", "down", 1))
    cp.wait_recv(("cross", "up", 2))
    right(1)
    left(1)
    left(2)
    hop(4)
    cp.wait_recv(("cross", "down", 2))
    cp.wait_recv(("cross", "up", 3))
    right(2)
    left(3)
    cp.wait_recv(("cross", "down", 3))
    cp.wait_recv(("cross", "down", 4))
    right(3)
    products(a_ref, b_ref, t_ref)
    turn(t_ref, tri, tri_l, tri_r)
    finish(x_ref, cot_ref, out_w, up_w, down_w, hs_ref, logit_ref, gate_ref, hg_ref, tri, tri_l, tri_r, out_ref, acc)

    total = acc[...]
    for stage, (group, place) in enumerate(((line, z * 2 + core), (plane, (xh * 2 + xl) * 4 + y))):
        slots[stage, place] = total
        ref = slots.at[stage, place]
        copies = []
        for n in range(1, 16):
            copy = pltpu.make_async_remote_copy(
                src_ref=ref,
                dst_ref=ref,
                send_sem=sum_send.at[stage, n],
                recv_sem=sum_recv.at[stage, n],
                device_id=group[n],
                device_id_type=MESH,
            )
            copy.start()
            copies.append(copy)
        for copy in copies:
            copy.wait_recv()
        total = jnp.sum(slots[stage], axis=0)
        for copy in copies:
            copy.wait_send()
    gate_out[...] = total[:3]
    hidden_out[...] = total[3:7]
    cp.wait_sends()
    assert cp.count == N_COPIES


VMEM = pl.BlockSpec(memory_space=pltpu.VMEM)
SMEM = pl.BlockSpec(memory_space=pltpu.SMEM)


def shards(pair_state, valid_tokens, proj_weight, gate_weight, out_weight, up_weight, down_weight, gate_scales, hidden_scales, cotangent):
    panel = pltpu.VMEM((16, BLK, BLK, C), BF16)
    edge = pltpu.VMEM((4, C * SA, 128), F32)
    positions = pltpu.VMEM((BLK * BLK, C), F32)
    layer_out, gate_grads, hidden_grads = pl.pallas_call(
        layer_kernel,
        out_shape=(
            jax.ShapeDtypeStruct((BLK, BLK, C), BF16),
            jax.ShapeDtypeStruct((3, C), F32),
            jax.ShapeDtypeStruct((4, C), F32),
        ),
        in_specs=[VMEM, SMEM] + [VMEM] * 8,
        out_specs=(VMEM, VMEM, VMEM),
        scratch_shapes=[
            panel, panel, edge, edge, pltpu.VMEM((C * ST, 128), F32), positions, positions, positions, positions, positions,
            pltpu.VMEM((BLK * BLK, 512), F32), pltpu.VMEM((8, C), F32),
            pltpu.VMEM((2 * C, C), BF16), pltpu.VMEM((2 * C, C), BF16), pltpu.VMEM((C, C), F32), pltpu.VMEM((C, C), F32),
            pltpu.VMEM((2, 16, 8, C), F32),
            pltpu.SemaphoreType.DMA((N_COPIES,)), pltpu.SemaphoreType.DMA((N_COPIES,)),
            pltpu.SemaphoreType.DMA((2, 16)), pltpu.SemaphoreType.DMA((2, 16)),
        ],
        compiler_params=pltpu.CompilerParams(collective_id=0, has_side_effects=True, vmem_limit_bytes=60 << 20),
        name="layer",
    )(pair_state, valid_tokens, proj_weight, gate_weight, out_weight, up_weight, down_weight, gate_scales, hidden_scales.reshape(1, 512), cotangent)
    return layer_out, gate_grads, hidden_grads.reshape(512)


def solution(mesh):
    return jax.shard_map(
        shards,
        mesh=mesh,
        in_specs=(P("row", "col", None), P(), P(), P(), P(), P(), P(), P(), P(), P("row", "col", None)),
        out_specs=(P("row", "col", None), P(), P()),
        check_vma=False,
    )
```

time: 140 us -> 84 us (0.60)
  Pallas kernels: 135 us -> 79.6 us
    pallas_call x1, Pallas kernels: 120 us -> 79.6 us  [shards(): pl.pallas_call(layer_kernel, out_shape=(jax.ShapeDtypeStruct((BLK, BLK, C...]
    pallas_call x1 -> x0, Pallas kernels: 15.5 us -> none  [shards(): pl.pallas_call(sum_kernel, out_shape=jax.ShapeDtypeStruct((8, C), F32), i...]
    unnamed x3 -> x7, local copies, waits for them, and re-layouts: 1.67 us -> 2.93 us
where the time goes in v2:
time: 84 us; the launch traced here: 83.8 us
  Pallas kernels  79.6 us (95%)
  local copies, waits for them, and re-layouts  2.93 us (3%)
  between operations  1.3 us (2%)
    pallas_call x1, Pallas kernels, shards(): pl.pallas_call(layer_kernel, out_shape=(jax.ShapeDtypeStruct((BLK, BLK, C...  79.6 us
    unnamed x7, local copies, waits for them, and re-layouts  2.93 us

profile of v2, /device:TPU:1, one launch (start us, length us, event | category | flops | bytes accessed | tf_op | source)
XLA Modules:
  0.0 83.8 jit_solution(6401009648757504775)
XLA Ops:
  1.3 79.6 %layer.1 = (bf16[32,32,128]{2,1,0:T(8,128)(2,1)}, f32[3,128]{1,0:T(4,128)}, f32[4,128]{1,0:T(4,128)}) custom-call(bf16[32,32,128]{2,1,0:T(8,128)(2,1)} %x_ref.1, s32[1]{0:T(128)S(6)} %copy.16.valid_ref, bf16[128,512]{1,0:T(8,128)(2,1)} %proj_w.1, bf16[128,128]{1,0:T(8,128)(2,1)} %gate_w.1, bf16[128,128]{1,0:T(8,128)(2,1)} %out_w.1, bf16[128,1024]{1,0:T(8,128)(2,1)} %up_w.1, ...), custom_call_target="tpu_custom_call" | custom-call | tf_op jit(solution)/shard_map/layer/pallas_call | solution.py:382
  80.9 0.0 copy-start.1
  80.9 1.7 %copy.17 = bf16[32,32,128]{2,1,0:T(8,128)(2,1)} copy(bf16[32,32,128]{2,1,0:T(8,128)(2,1)} %get-tuple-element.12) | data formatting | bytes 524288
  82.6 0.0 copy-done.1
  82.6 0.0 copy-start
  82.6 0.6 copy.18
  83.2 0.1 copy-done
  83.3 0.6 copy.19
Async XLA Ops:
  80.9 1.7 %copy-start.1 = (f32[3,128]{1,0:T(4,128)S(1)}, f32[3,128]{1,0:T(4,128)}, u32[]{:S(2)}) copy-start(f32[3,128]{1,0:T(4,128)} %get-tuple-element.13) | copy-start | bytes 4612
  82.6 0.7 copy-start

commit v3 on v2

v3 whole, which is shorter than its diff:
```python
import functools

import jax
import jax.numpy as jnp
from jax import lax
from jax.experimental import pallas as pl
from jax.experimental.pallas import tpu as pltpu
from jax.sharding import PartitionSpec as P

F32, BF16 = jnp.float32, jnp.bfloat16
EPS = 1e-5
MESH = pl.DeviceIdType.MESH
C = 128
BLK = 32
SA = 65
GROUP = 16
WIDE = 64
ST = 33


def mm(a, b):
    return jnp.dot(a, b, preferred_element_type=F32)


def mm_nt(a, b):
    return lax.dot_general(a, b, (((1,), (1,)), ((), ())), preferred_element_type=F32)


def sigmoid(v):
    return 0.5 * jnp.tanh(0.5 * v) + 0.5


def norm(v):
    centred = v - jnp.mean(v, axis=-1, keepdims=True)
    inverse = lax.rsqrt(jnp.mean(centred * centred, axis=-1, keepdims=True) + EPS)
    return centred * inverse, inverse


def norm_back(g, hat, inverse):
    g_mean = jnp.mean(g, axis=-1, keepdims=True)
    cross = jnp.mean(g * hat, axis=-1, keepdims=True)
    return inverse * (g - g_mean - hat * cross)


class Copies:
    def __init__(self, send, recv):
        self.send, self.recv, self.count, self.table = send, recv, 0, {}

    def start(self, name, src, dst, device, when=None):
        copy = pltpu.make_async_remote_copy(
            src_ref=src,
            dst_ref=dst,
            send_sem=self.send.at[self.count],
            recv_sem=self.recv.at[self.count],
            device_id=device,
            device_id_type=MESH,
        )
        self.count += 1
        self.table[name] = (copy, when)
        if when is None:
            copy.start()
        else:
            pl.when(when)(copy.start)

    def wait_recv(self, name):
        copy, when = self.table[name]
        if when is None:
            copy.wait_recv()
        else:
            pl.when(when)(copy.wait_recv)

    def wait_sends(self):
        for copy, when in self.table.values():
            if when is None:
                copy.wait_send()
            else:
                pl.when(when)(copy.wait_send)


PIECES = 4
CROSSING = (2, 3)
PIECE = BLK // PIECES
ITEMS = [(0, p) for p in CROSSING] + [(h, p) for h in range(2) for p in range(PIECES) if p not in CROSSING]
N_COPIES = 17 + 2 * PIECES + 7 * (len(ITEMS) + len(CROSSING))


def project(pan, blocks, quad, i, w_ref, s_ref, out):
    x = jnp.concatenate([pan[b, i + m] for m in range(GROUP) for b in blocks], axis=0)
    p = mm_nt(w_ref[...], x)
    for m in range(GROUP):
        value, logit = p[:C, m * 128 : (m + 1) * 128], p[C:, m * 128 : (m + 1) * 128]
        sig = 0.5 * jnp.tanh(s_ref[...] * logit) + 0.5
        proj = sig * value
        slope = proj * (logit * (1.0 - sig))
        out[quad, pl.ds(i + m, C, stride=SA), :] = proj
        out[quad, pl.ds(i + m + BLK, C, stride=SA), :] = slope


def products(a_ref, b_ref, t_ref, quads, first, last):
    def step(n, carry):
        for m in range(WIDE):
            ch = n * WIDE + m
            rows = pl.ds(ch * SA, 2 * BLK)
            a = jnp.concatenate([a_ref[q, rows, :].astype(BF16) for q in quads], axis=1)
            b = jnp.concatenate([b_ref[q, rows, :].astype(BF16) for q in quads], axis=1)
            t = mm_nt(a, b)
            t = jnp.concatenate([t[:BLK], t[BLK:]], axis=1)
            here = pl.ds(ch * ST, BLK)
            t_ref[here, :] = t if 0 in quads else t_ref[here, :] + t
        return carry

    lax.fori_loop(first, last, step, 0)


N_ROWS = 8
N_POS = N_ROWS * BLK


def parts_of(n):
    return pl.ds(n * N_ROWS, N_ROWS), pl.ds(pl.multiple_of(n * N_POS, N_POS), N_POS)


def early(x_ref, cot_ref, gate_w, down_w, gs_ref, logit_ref, gate_ref, hg_ref):
    gs = gs_ref[2:3, :]

    def chunk(n, carry):
        own, rows = parts_of(n)
        x = x_ref[own].reshape(N_POS, C).astype(F32)
        gate_logit = mm(norm(x)[0].astype(BF16), gate_w[...])
        logit_ref[rows, :] = gate_logit
        gate_ref[rows, :] = sigmoid(gs * gate_logit)
        hg_ref[rows, :] = mm_nt(cot_ref[own].reshape(N_POS, C), down_w[...])
        return carry

    lax.fori_loop(0, BLK // N_ROWS, chunk, 0)


def turn(t_ref, tri, tri_l, tri_r):
    def step(n, carry):
        for m in range(4):
            i = n * 4 + m
            t = t_ref[pl.ds(i, C, stride=ST), :].T
            rows = pl.ds(pl.multiple_of(i * BLK, BLK), BLK)
            tri[rows, :] = t[:BLK]
            tri_r[rows, :] = t[BLK : 2 * BLK]
            tri_l[rows, :] = t[2 * BLK : 3 * BLK]
        return carry

    lax.fori_loop(0, BLK // 4, step, 0)


def finish(x_ref, cot_ref, out_w, up_w, down_w, hs_ref, logit_ref, gate_ref, hg_ref, tri, tri_l, tri_r, acc):
    hs = hs_ref[...]
    x = x_ref[...].reshape(BLK * BLK, C).astype(F32)
    cot = cot_ref[...].reshape(BLK * BLK, C).astype(F32)
    gate_logit, gate, hidden_grad = logit_ref[...], gate_ref[...], hg_ref[...]
    tri_hat, tri_inv = norm(tri[...])
    out_proj = mm(tri_hat.astype(BF16), out_w[...])
    middle = (x + gate * out_proj).astype(BF16)
    mid_hat, mid_inv = norm(middle.astype(F32))
    upward = mm(mid_hat.astype(BF16), up_w[...])
    first, second = upward[:, :512], upward[:, 512:]
    s = sigmoid(first)
    act = first * s
    product = act * second
    hidden_term = jnp.sum(hidden_grad * product, axis=0, keepdims=True)
    scaled = hidden_grad * hs
    g_first = scaled * second * s * (1.0 + first * (1.0 - s))
    g_second = scaled * act
    g_up = jnp.concatenate([g_first.astype(BF16), g_second.astype(BF16)], axis=1)
    g_mid = cot + norm_back(mm_nt(g_up, up_w[...]), mid_hat, mid_inv)
    gate_term = jnp.sum(g_mid * out_proj * gate * (1.0 - gate) * gate_logit, axis=0, keepdims=True)
    g_out = (g_mid * gate).astype(BF16)
    t_grad = norm_back(mm_nt(g_out, out_w[...]), tri_hat, tri_inv).astype(BF16).astype(F32)
    left_term = jnp.sum(t_grad * tri_l[...], axis=0, keepdims=True)
    right_term = jnp.sum(t_grad * tri_r[...], axis=0, keepdims=True)
    parts = [left_term, right_term, gate_term] + [hidden_term[:, m * C : (m + 1) * C] for m in range(4)]
    acc[...] = jnp.concatenate(parts + [jnp.zeros((1, C), F32)], axis=0)
    return acc[...], middle, (hs * product).astype(BF16)


def layer_kernel(
    x_ref, valid_ref, proj_w, gate_w, out_w, up_w, down_w, gs_ref, hs_ref, cot_ref,
    out_ref, gate_out, hidden_out,
    lpan, rpan, a_ref, b_ref, t_ref, tri, tri_l, tri_r, logit_ref, gate_ref, hg_ref, acc, wa, wb, sa, sb, slots, out_buf,
    send, recv, sum_send, sum_recv, out_sem,
):
    r, c = lax.axis_index("row"), lax.axis_index("col")
    xh, z = r // 8, r % 8
    xl, y, core = c // 8, (c // 2) % 4, c % 2

    def row_of(h, dz):
        return h * 8 + (z + dz) % 8

    def col_of(h, dy, k):
        return (h * 4 + (y + dy) % 4) * 2 + k

    def slot_of(h, dz):
        return h * 8 + (z + dz + 8 - c % 8) % 8

    def col_at(slot):
        return slot // 8 * 8 + (slot + 2 * (c % 2)) % 4 * 2 + slot % 8 // 4

    own_slot = slot_of(xh, 0)
    above = (y + 2 * (z % 2)) % 4 + 4 * core
    to = (xl * 8 + (z + above) % 8, r)
    sent_slot = xl * 8 + above
    source = (c, col_at(own_slot))
    off = jnp.logical_or(c != r, own_slot % 8 != sent_slot % 8)

    far = (row_of(1 - xh, 0), c)
    up, down = (row_of(xh, 1), c), (row_of(xh, 7), c)
    sibling = (r, col_of(xl, 0, 1 - core))
    near = (r, col_of(1 - xl, 0, core))
    forth, back = (r, col_of(xl, 1, core)), (r, col_of(xl, 3, core))
    line = [(row_of(xh, dz), col_of(xl, 0, (core + dk) % 2)) for dz in range(8) for dk in range(2)]
    plane = [
        (row_of((xh + dh) % 2, 0), col_of((xl + dl) % 2, dy, core))
        for dh in range(2) for dl in range(2) for dy in range(4)
    ]

    barrier = pltpu.get_barrier_semaphore()
    for device in line[1:] + plane[1:]:
        pl.semaphore_signal(barrier, inc=1, device_id=device, device_id_type=MESH)

    @pl.when(off)
    def _():
        pl.semaphore_signal(barrier, inc=1, device_id=source, device_id_type=MESH)

    limit = valid_ref[0]
    rows_i = lax.broadcasted_iota(jnp.int32, (BLK, BLK, C), 0) + r * BLK
    rows_k = lax.broadcasted_iota(jnp.int32, (BLK, BLK, C), 1) + c * BLK
    keep = jnp.where(jnp.maximum(rows_i, rows_k) < limit, 1.0, 0.0)
    normed = (norm(x_ref[...].astype(F32))[0] * keep).astype(BF16)
    lpan[c] = normed

    @pl.when(jnp.logical_not(off))
    def _():
        rpan[own_slot] = normed

    pl.semaphore_wait(barrier, 30 + jnp.where(off, 1, 0))

    cp = Copies(send, recv)

    def part(p):
        return pl.ds(p * PIECE, PIECE)

    def r_copy(name, slot, p, device):
        ref = rpan.at[slot, part(p)]
        cp.start(name, ref, ref, device)

    def l_copy(name, slot, device):
        ref = lpan.at[slot]
        cp.start(name, ref, ref, device)

    def l_out(k, slot):
        l_copy(("forth", k), slot, forth)
        l_copy(("back", k), slot, back)

    def l_start():
        l_copy("near", c, near)
        l_out(0, c)
        l_copy("sib", c, sibling)

    pieces = [p for h, p in ITEMS if h == 0]
    for p in pieces:
        cp.start(("t", p), lpan.at[c, part(p)], rpan.at[sent_slot, part(p)], to, off)
    l_start()

    for w_ref, s_ref, side in ((wa, sa, 0), (wb, sb, 1)):
        w_ref[:C, :] = proj_w[:, side * C : (side + 1) * C].T
        w_ref[C:, :] = proj_w[:, (side + 2) * C : (side + 3) * C].T
        s_ref[...] = jnp.broadcast_to(0.5 * gs_ref[side : side + 1, :], (C, C)).T

    def last_hop(flow):
        return ITEMS[0::2] if flow == "up" else ITEMS[1::2]

    for p in pieces:
        cp.wait_recv(("t", p))
        if p not in CROSSING:
            r_copy(("far", p), own_slot, p, far)
        r_copy(("up", 1, (0, p)), own_slot, p, up)
        r_copy(("down", 1, (0, p)), own_slot, p, down)
    for h, p in ITEMS:
        if h:
            cp.wait_recv(("far", p))
            r_copy(("up", 1, (1, p)), slot_of(1 - xh, 0), p, up)
            r_copy(("down", 1, (1, p)), slot_of(1 - xh, 0), p, down)

    def l_near():
        cp.wait_recv("near")
        slot = col_of(1 - xl, 0, core)
        l_out(1, slot)
        l_copy("sibnear", slot, sibling)

    l_near()

    def hop(n, beside=()):
        for place, item in enumerate(ITEMS):
            for job, arguments in beside[place] if beside else ():
                job(*arguments)
            h, p = item
            for flow, sign, device in (("up", -1, up), ("down", 1, down)):
                if n == 4 and item not in last_hop(flow):
                    continue
                cp.wait_recv((flow, n, item))
                slot = slot_of(1 - xh if h else xh, sign * n + 8)
                if n < 3 or n == 3 and item in last_hop(flow):
                    r_copy((flow, n + 1, item), slot, p, device)
                if p in CROSSING:
                    r_copy(("cross", flow, n, p), slot, p, far)

    def crossed(flow, n):
        for p in CROSSING:
            if n < 4 or (0, p) in last_hop(flow):
                cp.wait_recv(("cross", flow, n, p))

    tops = (pl.ds(0, BLK // 2), pl.ds(BLK // 2, BLK // 2))

    def l_one(k):
        for n, (flow, dy, device) in enumerate((("forth", 3, forth), ("back", 1, back))):
            cp.wait_recv((flow, k))
            slot = col_of(1 - xl if k else xl, dy, core)
            ref = lpan.at[slot, tops[n]]
            cp.start((flow, k, "on"), ref, ref, device)
            l_copy(("sib", flow, k), slot, sibling)

    def l_two(k):
        for flow in ("forth", "back"):
            cp.wait_recv((flow, k, "on"))
        l_copy(("sib", "both", k), col_of(1 - xl if k else xl, 2, core), sibling)

    def l_end():
        for name in ["sib", "sibnear"] + [("sib", flow, k) for k in range(2) for flow in ("forth", "back", "both")]:
            cp.wait_recv(name)

    order = [0, 7, 1, 6, 2, 5, 3, 4]
    quads = [[slot_of(h, dz) for dz in order[2 * q : 2 * q + 2] for h in range(2)] for q in range(4)]

    def left(q, half):
        project(lpan, [col_at(slot) for slot in quads[q]], q, half * GROUP, wa, sa, a_ref)

    def right(q, half):
        project(rpan, quads[q], q, half * GROUP, wb, sb, b_ref)

    def triangle(qs, first, last):
        products(a_ref, b_ref, t_ref, qs, first, last)

    early(x_ref, cot_ref, gate_w, down_w, gs_ref, logit_ref, gate_ref, hg_ref)
    hop(1)
    for p in CROSSING:
        r_copy(("far", p), own_slot, p, far)
    l_one(0)
    hop(2)
    for p in CROSSING:
        cp.wait_recv(("far", p))
    crossed("up", 1)
    l_one(1)
    l_two(0)
    hop(3, ([], [(right, (0, 0))], [(right, (0, 1))], [(l_two, (1,)), (l_end, ()), (left, (0, 0))], [(left, (0, 1))], [(left, (1, 0))]))
    crossed("down", 1)
    crossed("up", 2)
    hop(4, (
        [], [], [(right, (1, 0)), (right, (1, 1))], [(left, (1, 1)), (left, (2, 0))],
        [(left, (2, 1))], [(left, (3, 0))],
    ))
    left(3, 1)
    crossed("down", 2)
    crossed("up", 3)
    right(2, 0)
    right(2, 1)
    crossed("down", 3)
    crossed("up", 4)
    crossed("down", 4)
    right(3, 0)
    right(3, 1)
    triangle((0, 1, 2, 3), 0, 2)
    turn(t_ref, tri, tri_l, tri_r)
    total, middle, hidden = finish(
        x_ref, cot_ref, out_w, up_w, down_w, hs_ref, logit_ref, gate_ref, hg_ref, tri, tri_l, tri_r, acc
    )

    for stage, (group, place) in enumerate(((line, z * 2 + core), (plane, (xh * 2 + xl) * 4 + y))):
        slots[stage, place] = total
        ref = slots.at[stage, place]
        copies = []
        for n in range(1, 16):
            copy = pltpu.make_async_remote_copy(
                src_ref=ref,
                dst_ref=ref,
                send_sem=sum_send.at[stage, n],
                recv_sem=sum_recv.at[stage, n],
                device_id=group[n],
                device_id_type=MESH,
            )
            copy.start()
            copies.append(copy)
        if stage == 0:
            layer_out = middle.astype(F32) + mm(hidden, down_w[...])
            out_ref[...] = layer_out.astype(BF16).reshape(BLK, BLK, C)
        for copy in copies:
            copy.wait_recv()
        total = jnp.sum(slots[stage], axis=0)
        for copy in copies:
            copy.wait_send()
    gate_out[...] = total[:3]
    hidden_out[...] = total[3:7]
    cp.wait_sends()
    assert cp.count == N_COPIES


VMEM = pl.BlockSpec(memory_space=pltpu.VMEM)
SMEM = pl.BlockSpec(memory_space=pltpu.SMEM)


def shards(pair_state, valid_tokens, proj_weight, gate_weight, out_weight, up_weight, down_weight, gate_scales, hidden_scales, cotangent):
    panel = pltpu.VMEM((16, BLK, BLK, C), BF16)
    edge = pltpu.VMEM((4, C * SA, 128), F32)
    positions = pltpu.VMEM((BLK * BLK, C), F32)
    layer_out, gate_grads, hidden_grads = pl.pallas_call(
        layer_kernel,
        out_shape=(
            jax.ShapeDtypeStruct((BLK, BLK, C), BF16),
            jax.ShapeDtypeStruct((3, C), F32),
            jax.ShapeDtypeStruct((4, C), F32),
        ),
        in_specs=[VMEM, SMEM] + [VMEM] * 8,
        out_specs=(VMEM, VMEM, VMEM),
        scratch_shapes=[
            panel, panel, edge, edge, pltpu.VMEM((C * ST, 128), F32), positions, positions, positions, positions, positions,
            pltpu.VMEM((BLK * BLK, 512), F32), pltpu.VMEM((8, C), F32),
            pltpu.VMEM((2 * C, C), BF16), pltpu.VMEM((2 * C, C), BF16), pltpu.VMEM((C, C), F32), pltpu.VMEM((C, C), F32),
            pltpu.VMEM((2, 16, 8, C), F32), pltpu.VMEM((BLK, BLK, C), BF16),
            pltpu.SemaphoreType.DMA((N_COPIES,)), pltpu.SemaphoreType.DMA((N_COPIES,)),
            pltpu.SemaphoreType.DMA((2, 16)), pltpu.SemaphoreType.DMA((2, 16)), pltpu.SemaphoreType.DMA,
        ],
        compiler_params=pltpu.CompilerParams(collective_id=0, has_side_effects=True, vmem_limit_bytes=60 << 20),
        name="layer",
    )(pair_state, valid_tokens, proj_weight, gate_weight, out_weight, up_weight, down_weight, gate_scales, hidden_scales.reshape(1, 512), cotangent)
    return layer_out, gate_grads, hidden_grads.reshape(512)


def solution(mesh):
    return jax.shard_map(
        shards,
        mesh=mesh,
        in_specs=(P("row", "col", None), P(), P(), P(), P(), P(), P(), P(), P(), P("row", "col", None)),
        out_specs=(P("row", "col", None), P(), P()),
        check_vma=False,
    )
```

time: 84 us -> 79.6 us (0.948)
  Pallas kernels: 79.6 us -> 75.2 us
    pallas_call x1, Pallas kernels: 79.6 us -> 75.2 us  [shards(): pl.pallas_call(layer_kernel, out_shape=(jax.ShapeDtypeStruct((BLK, BLK, C...]
where the time goes in v3:
time: 79.6 us; the launch traced here: 79.4 us
  Pallas kernels  75.2 us (94%)
  local copies, waits for them, and re-layouts  2.93 us (4%)
  between operations  1.3 us (2%)
    pallas_call x1, Pallas kernels, shards(): pl.pallas_call(layer_kernel, out_shape=(jax.ShapeDtypeStruct((BLK, BLK, C...  75.2 us
    unnamed x7, local copies, waits for them, and re-layouts  2.93 us

profile of v3, /device:TPU:1, one launch (start us, length us, event | category | flops | bytes accessed | tf_op | source)
XLA Modules:
  0.0 79.4 jit_solution(611605914278829544)
XLA Ops:
  1.3 75.2 %layer.1 = (bf16[32,32,128]{2,1,0:T(8,128)(2,1)}, f32[3,128]{1,0:T(4,128)}, f32[4,128]{1,0:T(4,128)}) custom-call(bf16[32,32,128]{2,1,0:T(8,128)(2,1)} %x_ref.1, s32[1]{0:T(128)S(6)} %copy.16.valid_ref, bf16[128,512]{1,0:T(8,128)(2,1)} %proj_w.1, bf16[128,128]{1,0:T(8,128)(2,1)} %gate_w.1, bf16[128,128]{1,0:T(8,128)(2,1)} %out_w.1, bf16[128,1024]{1,0:T(8,128)(2,1)} %up_w.1, ...), custom_call_target="tpu_custom_call" | custom-call | tf_op jit(solution)/shard_map/layer/pallas_call | solution.py:420
  76.5 0.0 copy-start.1
  76.5 1.7 %copy.17 = bf16[32,32,128]{2,1,0:T(8,128)(2,1)} copy(bf16[32,32,128]{2,1,0:T(8,128)(2,1)} %get-tuple-element.12) | data formatting | bytes 524288
  78.2 0.0 copy-done.1
  78.2 0.0 copy-start
  78.2 0.6 copy.18
  78.7 0.1 copy-done
  78.8 0.6 copy.19
Async XLA Ops:
  76.5 1.7 %copy-start.1 = (f32[3,128]{1,0:T(4,128)S(1)}, f32[3,128]{1,0:T(4,128)}, u32[]{:S(2)}) copy-start(f32[3,128]{1,0:T(4,128)} %get-tuple-element.13) | copy-start | bytes 4612
  78.2 0.7 copy-start

commit v4 on v3

--- a/solution.py
+++ b/solution.py
@@ -40,6 +40,12 @@
     g_mean = jnp.mean(g, axis=-1, keepdims=True)
     cross = jnp.mean(g * hat, axis=-1, keepdims=True)
     return inverse * (g - g_mean - hat * cross)
+
+
+FARTHEST = (
+    (8, 9, 6, 7, 10, 11, 4, 5, 12, 13, 2, 3, 14, 15, 1),
+    (10, 9, 11, 6, 14, 8, 5, 7, 13, 15, 2, 4, 12, 1, 3),
+)
 
 
 class Copies:
@@ -180,9 +186,10 @@
 
 
 def layer_kernel(
-    x_ref, valid_ref, proj_w, gate_w, out_w, up_w, down_w, gs_ref, hs_ref, cot_ref,
+    x_ref, valid_ref, proj_h, gate_h, out_h, up_h, down_h, gs_ref, hs_ref, cot_h,
     out_ref, gate_out, hidden_out,
     lpan, rpan, a_ref, b_ref, t_ref, tri, tri_l, tri_r, logit_ref, gate_ref, hg_ref, acc, wa, wb, sa, sb, slots, out_buf,
+    proj_w, gate_w, out_w, up_w, down_w, cot_ref, load_sem,
     send, recv, sum_send, sum_recv, out_sem,
 ):
     r, c = lax.axis_index("row"), lax.axis_index("col")
@@ -219,8 +226,17 @@
         for dh in range(2) for dl in range(2) for dy in range(4)
     ]
 
+    loads = [
+        pltpu.make_async_copy(src, dst, load_sem.at[n])
+        for n, (src, dst) in enumerate(
+            ((proj_h, proj_w), (gate_h, gate_w), (cot_h, cot_ref), (down_h, down_w), (out_h, out_w), (up_h, up_w))
+        )
+    ]
+    for load in loads:
+        load.start()
+
     barrier = pltpu.get_barrier_semaphore()
-    for device in line[1:] + plane[1:]:
+    for device in [line[n] for n in FARTHEST[0]] + [plane[n] for n in FARTHEST[1]]:
         pl.semaphore_signal(barrier, inc=1, device_id=device, device_id_type=MESH)
 
     @pl.when(off)
@@ -267,6 +283,8 @@
         cp.start(("t", p), lpan.at[c, part(p)], rpan.at[sent_slot, part(p)], to, off)
     l_start()
 
+    for load in loads:
+        load.wait()
     for w_ref, s_ref, side in ((wa, sa, 0), (wb, sb, 1)):
         w_ref[:C, :] = proj_w[:, side * C : (side + 1) * C].T
         w_ref[C:, :] = proj_w[:, (side + 2) * C : (side + 3) * C].T
@@ -380,11 +398,12 @@
         x_ref, cot_ref, out_w, up_w, down_w, hs_ref, logit_ref, gate_ref, hg_ref, tri, tri_l, tri_r, acc
     )
 
+    sent = []
     for stage, (group, place) in enumerate(((line, z * 2 + core), (plane, (xh * 2 + xl) * 4 + y))):
         slots[stage, place] = total
         ref = slots.at[stage, place]
         copies = []
-        for n in range(1, 16):
+        for n in FARTHEST[stage]:
             copy = pltpu.make_async_remote_copy(
                 src_ref=ref,
                 dst_ref=ref,
@@ -397,20 +416,32 @@
             copies.append(copy)
         if stage == 0:
             layer_out = middle.astype(F32) + mm(hidden, down_w[...])
-            out_ref[...] = layer_out.astype(BF16).reshape(BLK, BLK, C)
+            out_buf[...] = layer_out.astype(BF16).reshape(BLK, BLK, C)
+            out_copy = pltpu.make_async_copy(out_buf, out_ref, load_sem.at[6])
+            out_copy.start()
+            cp.wait_sends()
+        for copy in sent:
+            copy.wait_send()
         for copy in copies:
             copy.wait_recv()
         total = jnp.sum(slots[stage], axis=0)
-        for copy in copies:
-            copy.wait_send()
+        sent = copies
     gate_out[...] = total[:3]
     hidden_out[...] = total[3:7]
-    cp.wait_sends()
+    out_copy.wait()
+    for copy in sent:
+        copy.wait_send()
     assert cp.count == N_COPIES
 
 
 VMEM = pl.BlockSpec(memory_space=pltpu.VMEM)
+ANY = pl.BlockSpec(memory_space=pl.ANY)
 SMEM = pl.BlockSpec(memory_space=pltpu.SMEM)
+
+
+def hand_over(*refs):
+    for src, dst in zip(refs[:3], refs[3:]):
+        dst[...] = src[...]
 
 
 def shards(pair_state, valid_tokens, proj_weight, gate_weight, out_weight, up_weight, down_weight, gate_scales, hidden_scales, cotangent):
@@ -424,19 +455,28 @@
             jax.ShapeDtypeStruct((3, C), F32),
             jax.ShapeDtypeStruct((4, C), F32),
         ),
-        in_specs=[VMEM, SMEM] + [VMEM] * 8,
-        out_specs=(VMEM, VMEM, VMEM),
+        in_specs=[VMEM, SMEM] + [ANY] * 5 + [VMEM] * 2 + [ANY],
+        out_specs=(ANY, VMEM, VMEM),
         scratch_shapes=[
             panel, panel, edge, edge, pltpu.VMEM((C * ST, 128), F32), positions, positions, positions, positions, positions,
             pltpu.VMEM((BLK * BLK, 512), F32), pltpu.VMEM((8, C), F32),
             pltpu.VMEM((2 * C, C), BF16), pltpu.VMEM((2 * C, C), BF16), pltpu.VMEM((C, C), F32), pltpu.VMEM((C, C), F32),
             pltpu.VMEM((2, 16, 8, C), F32), pltpu.VMEM((BLK, BLK, C), BF16),
+            pltpu.VMEM((C, 4 * C), BF16), pltpu.VMEM((C, C), BF16), pltpu.VMEM((C, C), BF16), pltpu.VMEM((C, 1024), BF16),
+            pltpu.VMEM((512, C), BF16), pltpu.VMEM((BLK, BLK, C), BF16), pltpu.SemaphoreType.DMA((7,)),
             pltpu.SemaphoreType.DMA((N_COPIES,)), pltpu.SemaphoreType.DMA((N_COPIES,)),
             pltpu.SemaphoreType.DMA((2, 16)), pltpu.SemaphoreType.DMA((2, 16)), pltpu.SemaphoreType.DMA,
         ],
         compiler_params=pltpu.CompilerParams(collective_id=0, has_side_effects=True, vmem_limit_bytes=60 << 20),
         name="layer",
     )(pair_state, valid_tokens, proj_weight, gate_weight, out_weight, up_weight, down_weight, gate_scales, hidden_scales.reshape(1, 512), cotangent)
+    layer_out, gate_grads, hidden_grads = pl.pallas_call(
+        hand_over,
+        out_shape=tuple(jax.ShapeDtypeStruct(v.shape, v.dtype) for v in (layer_out, gate_grads, hidden_grads)),
+        in_specs=[VMEM] * 3,
+        out_specs=(VMEM,) * 3,
+        name="hand_over",
+    )(layer_out, gate_grads, hidden_grads)
     return layer_out, gate_grads, hidden_grads.reshape(512)
 
 

time: 79.6 us -> 77.3 us (0.971)
  local copies, waits for them, and re-layouts: 2.93 us -> 0 us
    unnamed x7 -> x0, local copies, waits for them, and re-layouts: 2.93 us -> none
    pallas_call x0 -> x1, Pallas kernels: none -> 1.68 us  [shards(): pl.pallas_call(hand_over, out_shape=tuple((jax.ShapeDtypeStruct(v.shape,...]
    pallas_call x1, Pallas kernels: 75.2 us -> 74.2 us  [shards(): pl.pallas_call(layer_kernel, out_shape=(jax.ShapeDtypeStruct((BLK, BLK, C...]
where the time goes in v4:
time: 77.3 us; the launch traced here: 77.2 us
  Pallas kernels  75.9 us (98%)
  between operations  1.29 us (2%)
    pallas_call x1, Pallas kernels, shards(): pl.pallas_call(layer_kernel, out_shape=(jax.ShapeDtypeStruct((BLK, BLK, C...  74.2 us
    pallas_call x1, Pallas kernels, shards(): pl.pallas_call(hand_over, out_shape=tuple((jax.ShapeDtypeStruct(v.shape,...  1.68 us

profile of v4, /device:TPU:1, one launch (start us, length us, event | category | flops | bytes accessed | tf_op | source)
XLA Modules:
  0.0 77.2 jit_solution(4924312269754141424)
XLA Ops:
  1.3 74.2 %layer.1 = (bf16[32,32,128]{2,1,0:T(8,128)(2,1)}, f32[3,128]{1,0:T(4,128)}, f32[4,128]{1,0:T(4,128)}) custom-call(bf16[32,32,128]{2,1,0:T(8,128)(2,1)} %x_ref.1, s32[1]{0:T(128)S(6)} %copy.13.valid_ref, bf16[128,512]{1,0:T(8,128)(2,1)} %proj_h.1, bf16[128,128]{1,0:T(8,128)(2,1)} %gate_h.1, bf16[128,128]{1,0:T(8,128)(2,1)} %out_h.1, bf16[128,1024]{1,0:T(8,128)(2,1)} %up_h.1, ...), custom_call_target="tpu_custom_call" | custom-call | tf_op jit(solution)/shard_map/layer/pallas_call | solution.py:451
  75.5 1.7 %hand_over.1 = (bf16[32,32,128]{2,1,0:T(8,128)(2,1)}, f32[3,128]{1,0:T(4,128)}, f32[4,128]{1,0:T(4,128)}) custom-call(bf16[32,32,128]{2,1,0:T(8,128)(2,1)} %get-tuple-element.9.refs_0_, f32[3,128]{1,0:T(4,128)} %get-tuple-element.10.refs_1_, f32[4,128]{1,0:T(4,128)} %get-tuple-element.11.refs_2_), custom_call_target="tpu_custom_call" | custom-call | tf_op jit(solution)/shard_map/hand_over/pallas_call | solution.py:473

commit v5 on v4

--- a/solution.py
+++ b/solution.py
@@ -143,8 +143,8 @@
 
 def turn(t_ref, tri, tri_l, tri_r):
     def step(n, carry):
-        for m in range(4):
-            i = n * 4 + m
+        for m in range(16):
+            i = n * 16 + m
             t = t_ref[pl.ds(i, C, stride=ST), :].T
             rows = pl.ds(pl.multiple_of(i * BLK, BLK), BLK)
             tri[rows, :] = t[:BLK]
@@ -152,7 +152,7 @@
             tri_l[rows, :] = t[2 * BLK : 3 * BLK]
         return carry
 
-    lax.fori_loop(0, BLK // 4, step, 0)
+    lax.fori_loop(0, BLK // 16, step, 0)
 
 
 def finish(x_ref, cot_ref, out_w, up_w, down_w, hs_ref, logit_ref, gate_ref, hg_ref, tri, tri_l, tri_r, acc):

time: 77.3 us -> 77 us (level)
  no operation moved by 1% of the time
where the time goes in v5:
time: 77 us; the launch traced here: 76.8 us
  Pallas kernels  75.6 us (98%)
  between operations  1.29 us (2%)
    pallas_call x1, Pallas kernels, shards(): pl.pallas_call(layer_kernel, out_shape=(jax.ShapeDtypeStruct((BLK, BLK, C...  73.9 us
    pallas_call x1, Pallas kernels, shards(): pl.pallas_call(hand_over, out_shape=tuple((jax.ShapeDtypeStruct(v.shape,...  1.68 us

profile of v5, /device:TPU:1, one launch (start us, length us, event | category | flops | bytes accessed | tf_op | source)
XLA Modules:
  0.0 76.8 jit_solution(11444665379413341202)
XLA Ops:
  1.3 73.9 %layer.1 = (bf16[32,32,128]{2,1,0:T(8,128)(2,1)}, f32[3,128]{1,0:T(4,128)}, f32[4,128]{1,0:T(4,128)}) custom-call(bf16[32,32,128]{2,1,0:T(8,128)(2,1)} %x_ref.1, s32[1]{0:T(128)S(6)} %copy.13.valid_ref, bf16[128,512]{1,0:T(8,128)(2,1)} %proj_h.1, bf16[128,128]{1,0:T(8,128)(2,1)} %gate_h.1, bf16[128,128]{1,0:T(8,128)(2,1)} %out_h.1, bf16[128,1024]{1,0:T(8,128)(2,1)} %up_h.1, ...), custom_call_target="tpu_custom_call" | custom-call | tf_op jit(solution)/shard_map/layer/pallas_call | solution.py:451
  75.2 1.7 %hand_over.1 = (bf16[32,32,128]{2,1,0:T(8,128)(2,1)}, f32[3,128]{1,0:T(4,128)}, f32[4,128]{1,0:T(4,128)}) custom-call(bf16[32,32,128]{2,1,0:T(8,128)(2,1)} %get-tuple-element.9.refs_0_, f32[3,128]{1,0:T(4,128)} %get-tuple-element.10.refs_1_, f32[4,128]{1,0:T(4,128)} %get-tuple-element.11.refs_2_), custom_call_target="tpu_custom_call" | custom-call | tf_op jit(solution)/shard_map/hand_over/pallas_call | solution.py:473
